TPU v7x, 128 devices: a whole 4x4x4 slice. The times are simulated.
128 devices in a mesh: strip: 4 (over x), tile: 32 (over z, y, core).
Axes of the slice: x: 4, y: 4, z: 4, core: 2. Of those that a mesh axis runs over, the one named last changes fastest.
Arguments:
- num_coef: bfloat16 [40, 65536], P(None, ('strip', 'tile')), may hold values from -1.25 to 1.25
- den_coef: bfloat16 [38, 65536], P(None, ('strip', 'tile')), may hold values from -0.039794922 to 0.039794922
- bias: float32 [6, 65536], P(None, ('strip', 'tile')), may hold values from -3 to 3
- scene_chain: int32 [65536], P(('strip', 'tile')), may hold values from 0 to 65535, as said below
- bucket_scenes: int32 [128, 1024], P(('strip', 'tile')), may hold values from 0 to 511
- tie_counts: int32 [128, 128], P(('strip', 'tile')), may hold values from 1 to 256, as said below
- tie_obs: float32 [2, 4194304], P(None, ('strip', 'tile')), may hold values from -1 to 1
- tie_prior: float32 [4194304], P(('strip', 'tile')), may hold values from 0.5 to 2
- tie_pick: int32 [4194304], P(('strip', 'tile')), may hold values from 0 to 7
- tie_point: int32 [4194304], P(('strip', 'tile')), may hold values from 0 to 2047
- ground: float32 [3, 262144], P(None, ('strip', 'tile')), may hold values from -1 to 1
Outputs:
- ground_next: float32 [3, 262144], P(None, ('strip', 'tile'))
- bias_step: float32 [6, 65536], P(None, ('strip', 'tile'))
Inputs may be any that keep to these rules, and one draw needn't show every extreme that they name: The first tie_counts[d, e] of the 256 slots that device d holds for device e (its slots e * 256 to (e + 1) * 256 - 1) carry ties; the others are empty. `scene_chain`: each number appears once; strip s holds positions s * 16384 to (s + 1) * 16384 - 1 in along-track order. Scene j of the device with tile index t has its position in strip j // 128, within t * 512 to (t + 1) * 512 - 1 of that strip's positions. `bucket_scenes`: row d, entries e * 8 to (e + 1) * 8 - 1: local scenes of device d seen from the ground tiles of device e.
All inputs are finite; a program needn't handle non-finite values.
Results may differ from a plain program's by a relative error of at most 0.0003.
Values may be sent and summed in bfloat16 or wider, within the bound.
No kernel may reach another device: no remote copies, remote signals or barrier semaphores. Data moves between devices by JAX's collectives and lax.ppermute only.
A program may use at most 128 MiB of HBM per device.

v0:
```python
import functools

import jax
import jax.numpy as jnp
from jax import lax
from jax.experimental import pallas as pl
from jax.experimental.pallas import tpu as pltpu
from jax.sharding import PartitionSpec as P

SWEEPS = 4
AXES = ("strip", "tile")
F32 = jnp.float32
BF16 = jnp.bfloat16
I32 = jnp.int32
LANES = 128
SUB = 8

cauchy_scale = 1.0
point_damping = 1.0
smooth_gain = 0.25

LATE_TERMS = 64
BIAS_ROW = 80
CHAIN_ROW = 104
CHAIN_SENT = 88
SCENE_ROWS = 6
BUCKET_ROWS = 8 + SCENE_ROWS
SCENE_LANES = 16
POS_LANE = 12
HALO = SWEEPS - 1
PART_ROWS = 32


def lane_iota(shape):
    return lax.broadcasted_iota(I32, shape, len(shape) - 1)


def sublane_iota(shape):
    return lax.broadcasted_iota(I32, shape, len(shape) - 2)


def split3(value):
    high = value.astype(BF16).astype(F32)
    rest = value - high
    middle = rest.astype(BF16).astype(F32)
    return high, middle, rest - middle


def take_lanes(table, lanes):
    return jnp.take_along_axis(table, lanes, axis=1, mode="promise_in_bounds")


def inverse_sym(matrix):
    cofactor = [
        matrix[3] * matrix[5] - matrix[4] * matrix[4],
        matrix[2] * matrix[4] - matrix[1] * matrix[5],
        matrix[1] * matrix[4] - matrix[2] * matrix[3],
        matrix[0] * matrix[5] - matrix[2] * matrix[2],
        matrix[1] * matrix[2] - matrix[0] * matrix[4],
        matrix[0] * matrix[3] - matrix[1] * matrix[1],
    ]
    determinant = matrix[0] * cofactor[0] + matrix[1] * cofactor[1] + matrix[2] * cofactor[2]
    return [cofactor_entry / determinant for cofactor_entry in cofactor]


def apply_sym(inverse, comp_one, comp_two, comp_three):
    return [
        inverse[0] * comp_one + inverse[1] * comp_two + inverse[2] * comp_three,
        inverse[1] * comp_one + inverse[3] * comp_two + inverse[4] * comp_three,
        inverse[2] * comp_one + inverse[4] * comp_two + inverse[5] * comp_three,
    ]


def pack_kernel(
    num_hbm,
    den_hbm,
    bias_hbm,
    chain_hbm,
    list_hbm,
    counts_hbm,
    obs_hbm,
    prior_hbm,
    pick_hbm,
    point_hbm,
    out_ref,
    num_ref,
    den_ref,
    bias_ref,
    chain_ref,
    list_ref,
    counts_ref,
    obs_ref,
    prior_ref,
    pick_ref,
    point_ref,
    table_ref,
    listed_ref,
    sems,
):
    copies = [
        pltpu.make_async_copy(source, target, sems.at[index])
        for index, (source, target) in enumerate(
            [
                (num_hbm, num_ref),
                (den_hbm, den_ref),
                (bias_hbm, bias_ref),
                (chain_hbm, chain_ref),
                (list_hbm, list_ref),
                (counts_hbm, counts_ref),
                (obs_hbm, obs_ref),
                (prior_hbm, prior_ref),
                (pick_hbm, pick_ref),
                (point_hbm, point_ref),
            ]
        )
    ]
    for copy in copies:
        copy.start()
    owners = out_ref.shape[0] // BUCKET_ROWS
    scenes = num_ref.shape[1]
    listed = list_ref.shape[1]
    table_ref[...] = jnp.zeros(table_ref.shape, F32)
    for copy in copies[:5]:
        copy.wait()
    numer = num_ref[...].astype(F32)
    denom = den_ref[...].astype(F32)
    for which in range(2):
        table_ref[16 * which : 16 * which + 16, :] = numer[20 * which : 20 * which + 16]
        table_ref[33 + 16 * which : 48 + 16 * which, :] = denom[19 * which : 19 * which + 15]
        late = LATE_TERMS + 4 * which
        table_ref[late : late + 4, :] = numer[20 * which + 16 : 20 * which + 20]
        table_ref[late + 8 : late + 12, :] = denom[19 * which + 15 : 19 * which + 19]
    for part, value in enumerate(split3(bias_ref[...])):
        first = BIAS_ROW + part * SUB
        table_ref[first : first + 6, :] = value
    place = (chain_ref[...] & (scenes - 1)) + (lane_iota((1, scenes)) // (scenes // 4)) * scenes
    table_ref[CHAIN_ROW : CHAIN_ROW + 1, :] = (place >> 8).astype(F32)
    table_ref[CHAIN_ROW + 1 : CHAIN_ROW + 2, :] = (place & 255).astype(F32)
    table = table_ref[...].astype(BF16)
    for first in range(0, listed, 256):
        chosen = jnp.broadcast_to(list_ref[:, first : first + 256], (scenes, 256))
        onehot = jnp.where(chosen == sublane_iota((scenes, 256)), 1.0, 0.0).astype(BF16)
        got = jnp.dot(table, onehot, preferred_element_type=F32)
        bias_rows = sum(
            got[BIAS_ROW + part * SUB : BIAS_ROW + (part + 1) * SUB] for part in range(1, 3)
        ) + got[BIAS_ROW : BIAS_ROW + SUB]
        got = jnp.concatenate([got[:BIAS_ROW], bias_rows, got[CHAIN_ROW:]], axis=0)
        got = jnp.concatenate([got, jnp.zeros((LANES - got.shape[0], 256), F32)], axis=0)
        for part in range(0, 256, LANES):
            listed_ref[first + part : first + part + LANES, :] = got[:, part : part + LANES].T
    for copy in copies[5:]:
        copy.wait()
    counts = jnp.broadcast_to(counts_ref[...].astype(F32), (owners, owners)).T
    slot = lane_iota((SUB, LANES)).astype(F32)
    lane = lane_iota((SUB, LANES))
    for group in range(owners // SUB):
        live_count = counts[group * SUB : (group + 1) * SUB, :1]
        base = group * SUB * BUCKET_ROWS

        def put(row, value):
            out_ref[pl.ds(base + row, SUB, stride=BUCKET_ROWS), :] = value

        for row in range(4):
            put(row, obs_ref[pl.ds(group * SUB * 4 + row, SUB, stride=4), :])
        for half in range(2):
            rows = pl.ds(group * SUB * 2 + half, SUB, stride=2)
            live = slot + float(half * LANES) < live_count
            put(4 + half, jnp.where(live, prior_ref[rows, :], 0.0))
            put(6 + half, (pick_ref[rows, :] * 2048 + point_ref[rows, :]).astype(F32))
        blocks = [listed_ref[pl.ds(group * SUB * 8 + k, SUB, stride=8), :] for k in range(8)]
        for bit in range(3):
            step = 1 << bit
            shift = step * SCENE_LANES
            odd = ((lane // SCENE_LANES) & step) != 0
            turned = list(blocks)
            for k in range(8):
                if k & step:
                    continue
                low, high = blocks[k], blocks[k + step]
                turned[k] = jnp.where(odd, pltpu.roll(high, shift, 1), low)
                turned[k + step] = jnp.where(odd, high, pltpu.roll(low, LANES - shift, 1))
            blocks = turned
        for block in range(SCENE_ROWS):
            put(8 + block, blocks[block])


def ratios(coef, east, north, up):
    east_sq, north_sq, up_sq = east * east, north * north, up * up
    east_north, east_up, north_up = east * north, east * up, north * up
    terms = [
        (1, None, None, None),
        (east, 1, None, None),
        (north, None, 1, None),
        (up, None, None, 1),
        (east_north, north, east, None),
        (east_up, up, None, east),
        (north_up, None, up, north),
        (east_sq, 2.0 * east, None, None),
        (north_sq, None, 2.0 * north, None),
        (up_sq, None, None, 2.0 * up),
        (east_north * up, north_up, east_up, east_north),
        (east_sq * east, 3.0 * east_sq, None, None),
        (east * north_sq, north_sq, 2.0 * east_north, None),
        (east * up_sq, up_sq, None, 2.0 * east_up),
        (east_sq * north, 2.0 * east_north, east_sq, None),
        (north_sq * north, None, 3.0 * north_sq, None),
        (north * up_sq, None, up_sq, 2.0 * north_up),
        (east_sq * up, 2.0 * east_up, None, east_sq),
        (north_sq * up, None, 2.0 * north_up, north_sq),
        (up_sq * up, None, None, 3.0 * up_sq),
    ]
    sums = [[None] * 4 for _ in range(4)]
    for cubic in (2, 3):
        sums[cubic][0] = jnp.ones_like(east)

    def add(cubic, term, row):
        if cubic >= 2 and term == 0:
            return
        value = coef(row)
        for which, factor in enumerate(terms[term]):
            if factor is None:
                continue
            product = value if isinstance(factor, int) else value * factor
            held = sums[cubic][which]
            sums[cubic][which] = product if held is None else held + product

    bias = []
    for word in range(SCENE_LANES):
        for cubic in range(4):
            add(cubic, word, cubic * SCENE_LANES + word)
        add(word // 4, 16 + word % 4, LATE_TERMS + word)
        if word < 6:
            bias.append(coef(BIAS_ROW + word))
    found = []
    for top, bottom in ((sums[0], sums[2]), (sums[1], sums[3])):
        quotient = top[0] / bottom[0]
        found.append(quotient)
        found.append(
            [(top[which] - quotient * bottom[which]) / bottom[0] for which in range(1, 4)]
        )
    return found, bias


def tile_kernel(
    got_ref,
    ground_ref,
    next_ref,
    out_ref,
    packed_ref,
    parts_even,
    parts_odd,
    sums_ref,
    table_ref,
    step_ref,
    total_ref,
    place_ref,
    halo_ref,
    coef_ref,
    *,
    strips,
):
    owners = got_ref.shape[0] // BUCKET_ROWS
    groups = owners // SUB
    tiles = owners // strips
    points = ground_ref.shape[1]
    point_rows = points // LANES
    vreg = (SUB, LANES)
    lane = lane_iota(vreg)

    def fill_table(value):
        for axis in range(3):
            for row in range(point_rows):
                at = (axis * point_rows + row) * SUB
                table_ref[at : at + SUB, :] = jnp.broadcast_to(value(axis, row), vreg)

    fill_table(lambda axis, row: ground_ref[axis : axis + 1, row * LANES : (row + 1) * LANES])

    def tie_row(group, row):
        return got_ref[pl.ds(group * (SUB * BUCKET_ROWS) + row, SUB, stride=BUCKET_ROWS), :]

    def code_of(group, half):
        code = tie_row(group, 6 + half).astype(I32)
        return code >> 11, code & (points - 1)

    def gather_points(point):
        high = point >> 7
        low = point & (LANES - 1)
        found = [None] * 3
        for row in range(point_rows):
            here = high == row
            for axis in range(3):
                at = (axis * point_rows + row) * SUB
                value = take_lanes(table_ref[at : at + SUB, :], low)
                found[axis] = value if row == 0 else jnp.where(here, value, found[axis])
        return found

    def turn_scenes(group):
        for block in range(SCENE_ROWS):
            value = tie_row(group, 8 + block)
            for word in range(SCENE_LANES if block < 5 else 6):
                at = (block * SCENE_LANES + word) * SUB
                coef_ref[at : at + SUB, :] = (
                    pltpu.roll(value, LANES - word, 1) if word else value
                )

    def first_pass(group, half, parts_ref):
        pick, point = code_of(group, half)
        first_lane = pick * SCENE_LANES
        east, north, up = gather_points(point)

        def coef(row):
            return take_lanes(coef_ref[row * SUB : (row + 1) * SUB, :], first_lane)

        line_obs = tie_row(group, 2 * half)
        samp_obs = tie_row(group, 2 * half + 1)
        prior = tie_row(group, 4 + half)
        (line_ratio, line_jac, samp_ratio, samp_jac), bias = ratios(coef, east, north, up)
        line_res = line_obs - (line_ratio + bias[0] + bias[1] * samp_obs + bias[2] * line_obs)
        samp_res = samp_obs - (samp_ratio + bias[3] + bias[4] * samp_obs + bias[5] * line_obs)
        weight = prior / (1.0 + (line_res * line_res + samp_res * samp_res) / cauchy_scale)
        place = pl.ds((group * 2 + half) * SUB, SUB)
        for row, value in enumerate([line_res, samp_res] + line_jac + samp_jac + [weight]):
            packed_ref[row, place, :] = value
        pairs = [(0, 0), (0, 1), (0, 2), (1, 1), (1, 2), (2, 2)]
        sums = [weight * (line_jac[a] * line_jac[b] + samp_jac[a] * samp_jac[b]) for a, b in pairs]
        sums += [weight * (line_jac[a] * line_res + samp_jac[a] * samp_res) for a in range(3)]

        def put(row, value):
            parts_ref[pl.ds(half * PART_ROWS + row, SUB, stride=2 * PART_ROWS), :] = value

        for row, value in enumerate(sums):
            for part, piece in enumerate(split3(value)):
                put(row * 3 + part, piece)
        put(27, (point >> 8).astype(F32))
        put(28, (point & 255).astype(F32))

    wide = (16, LANES)
    steps_iota = [
        (sublane_iota(wide) + 16 * row).astype(F32).astype(BF16) for row in range(16)
    ]
    one = jnp.ones(wide, BF16)
    zero = jnp.zeros(wide, BF16)

    def sum_pass(first_bucket, count, parts_ref):
        left = []
        right = []
        for bucket in range(first_bucket, first_bucket + count):
            for half in range(2):
                first = (bucket * 2 + half) * PART_ROWS
                values = parts_ref[first : first + PART_ROWS, :].astype(BF16)
                high = jnp.broadcast_to(parts_ref[first + 27 : first + 28, :], wide).astype(BF16)
                low = jnp.broadcast_to(parts_ref[first + 28 : first + 29, :], wide).astype(BF16)
                rows = []
                for index in range(8):
                    here = high == jnp.full(wide, index, BF16)
                    rows.append(jnp.where(here, values[:16], zero))
                    rows.append(jnp.where(here, values[16:], zero))
                left.append(jnp.concatenate(rows, axis=0))
                right.append(
                    jnp.concatenate(
                        [jnp.where(low == step, one, zero) for step in steps_iota], axis=0
                    )
                )
        product = lax.dot_general(
            jnp.concatenate(left, axis=1),
            jnp.concatenate(right, axis=1),
            (((1,), (1,)), ((), ())),
            preferred_element_type=F32,
        )
        for half in range(2):
            sums_ref[half] += product[:, half * LANES : (half + 1) * LANES]

    def both(group, lagging, parts_ref, lagging_ref):
        if group is not None:
            turn_scenes(group)
        for half in range(2):
            if lagging:
                sum_pass(half * 4, 4, lagging_ref)
            if group is not None:
                first_pass(group, half, parts_ref)

    for ref in (parts_even, parts_odd):
        ref[...] = jnp.zeros(ref.shape, F32)
    sums_ref[...] = jnp.zeros(sums_ref.shape, F32)
    both(0, False, parts_even, None)

    def pair_of_groups(pair, carry):
        both(2 * pair + 1, True, parts_odd, parts_even)
        both(2 * pair + 2, True, parts_even, parts_odd)
        return carry

    lax.fori_loop(0, groups // 2 - 1, pair_of_groups, 0)
    both(groups - 1, True, parts_odd, parts_even)
    both(None, True, None, parts_odd)

    def point_sum(row, half):
        return sum(
            sums_ref[half, pl.ds(row * 3 + part, SUB, stride=PART_ROWS), :] for part in (2, 1, 0)
        )

    for half in range(2):
        sums = [point_sum(row, half) for row in range(9)]
        matrix = [
            sums[0] + point_damping,
            sums[1],
            sums[2],
            sums[3] + point_damping,
            sums[4],
            sums[5] + point_damping,
        ]
        steps = apply_sym(inverse_sym(matrix), sums[6], sums[7], sums[8])
        for axis in range(3):
            step_ref[pl.ds(axis * point_rows + half, SUB, stride=2), :] = steps[axis]
    for axis in range(3):
        for row in range(point_rows):
            columns = slice(row * LANES, (row + 1) * LANES)
            at = axis * point_rows + row
            next_ref[axis : axis + 1, columns] = (
                ground_ref[axis : axis + 1, columns] + step_ref[at : at + 1, :]
            )
    fill_table(
        lambda axis, row: step_ref[axis * point_rows + row : axis * point_rows + row + 1, :]
    )

    def second_pass(group, carry):
        rows = []
        picks = []
        for half in range(2):
            pick, point = code_of(group, half)
            tie_step = gather_points(point)
            place = pl.ds((group * 2 + half) * SUB, SUB)
            packed = [packed_ref[row, place, :] for row in range(9)]
            line_obs = tie_row(group, 2 * half)
            samp_obs = tie_row(group, 2 * half + 1)
            weight = packed[8]
            line_res = packed[0] - (
                packed[2] * tie_step[0] + packed[3] * tie_step[1] + packed[4] * tie_step[2]
            )
            samp_res = packed[1] - (
                packed[5] * tie_step[0] + packed[6] * tie_step[1] + packed[7] * tie_step[2]
            )
            samp_weight = weight * samp_obs
            line_weight = weight * line_obs
            rows.append(
                [
                    weight,
                    samp_weight,
                    line_weight,
                    samp_weight * samp_obs,
                    samp_weight * line_obs,
                    line_weight * line_obs,
                    weight * line_res,
                    samp_weight * line_res,
                    line_weight * line_res,
                    weight * samp_res,
                    samp_weight * samp_res,
                    line_weight * samp_res,
                ]
            )
            picks.append(pick)
        total = jnp.zeros(vreg, F32)
        for scene in range(8):
            first, second = picks[0] == scene, picks[1] == scene
            for row in range(12):
                value = jnp.where(first, rows[0][row], 0.0) + jnp.where(second, rows[1][row], 0.0)
                total = jnp.where(
                    lane == scene * SCENE_LANES + row,
                    jnp.sum(value, axis=1, keepdims=True),
                    total,
                )
        place = pl.ds(group * SUB, SUB)
        total_ref[place, :] = total
        chain = tie_row(group, 8 + CHAIN_SENT // SCENE_LANES)
        chain_lane = (lane // SCENE_LANES) * SCENE_LANES + CHAIN_SENT % SCENE_LANES
        place_ref[place, :] = take_lanes(chain, chain_lane) * 256.0 + take_lanes(
            chain, chain_lane + 1
        )
        return carry

    lax.fori_loop(0, groups, second_pass, 0, unroll=2)

    segment = 4 * LANES
    word = lane % SCENE_LANES
    stacked = []
    for near in range(HALO):
        rows = []
        for strip in range(strips):
            for side in range(2):
                at = float(strip * segment + (near if side else segment - HALO + near))
                for block in range(0, tiles, SUB):
                    here = [pl.ds(s * tiles + block, SUB) for s in range(strips)]
                    rows.append(
                        sum(jnp.where(place_ref[h, :] == at, total_ref[h, :], 0.0) for h in here)
                    )
        stacked.append(jnp.concatenate(rows, axis=0))
    stacked = jnp.concatenate(stacked, axis=1)
    source = sublane_iota((HALO * LANES, 2 * LANES))
    target = lane_iota((HALO * LANES, 2 * LANES))
    chosen = (source % SCENE_LANES == target // SCENE_LANES) & (
        target % SCENE_LANES == source // LANES + POS_LANE + 1
    )
    chosen = jnp.where(chosen, 1.0, 0.0).astype(BF16)
    moved = sum(
        jnp.dot(part.astype(BF16), chosen, preferred_element_type=F32)
        for part in reversed(split3(stacked))
    )
    flag = lane // SCENE_LANES == 4
    for side in range(2):
        for part in range(2):
            for strip in range(strips):
                slot = strip * 4 + side * 2 + part
                edge = tiles if side else SUB
                halo_ref[slot, edge : edge + SUB, :] = jnp.zeros(vreg, F32)
                for block in range(0, tiles, SUB):
                    at = (strip * 2 + side) * tiles + block
                    value = moved[at : at + SUB, part * LANES : (part + 1) * LANES]
                    if part:
                        value = jnp.where(flag, 1.0, value)
                    first = SUB + block + (-1 if side else 1)
                    halo_ref[slot, first : first + SUB, :] = value
    for strip in range(strips):
        start = float(strip * segment)
        for block in range(0, tiles, SUB):
            for source in range(strips):
                place = place_ref[pl.ds(source * tiles + block, SUB), :] - start
                inside = (place >= 0.0) & (place < float(segment))
                value = total_ref[pl.ds(source * tiles + block, SUB), :]
                value = jnp.where(word == POS_LANE, jnp.where(inside, place, -1.0), value)
                value = jnp.where(
                    word > POS_LANE,
                    halo_ref[strip * 4 + source, SUB + block : 2 * SUB + block, :],
                    value,
                )
                out_ref[
                    pl.ds((strip * tiles + block) * strips + source, SUB, stride=strips), :
                ] = value


def chain_kernel(got_ref, out_ref, turned_ref, *, coupling):
    scenes = out_ref.shape[1]
    total = jnp.zeros((3 * SCENE_LANES, scenes), F32)
    border = jnp.zeros((SUB, LANES), F32)
    for first in range(0, got_ref.shape[0], LANES):
        block = got_ref[first : first + LANES, :]
        for row in range(0, LANES, SUB):
            border = border + block[row : row + SUB]
        turned = block.T
        values = jnp.concatenate(
            [turned[k * SCENE_LANES : (k + 1) * SCENE_LANES] for k in range(8)], axis=1
        )
        position = values[POS_LANE : POS_LANE + 1].astype(I32)
        onehot = jnp.where(
            jnp.broadcast_to(position, (scenes, 8 * LANES)) == sublane_iota((scenes, 8 * LANES)),
            1.0,
            0.0,
        ).astype(BF16)
        pieces = jnp.concatenate(split3(values), axis=0).astype(BF16)
        total = total + lax.dot_general(
            pieces, onehot, (((1,), (1,)), ((), ())), preferred_element_type=F32
        )
    sums = total[32:48] + total[16:32] + total[:16]
    sums = jnp.where(sublane_iota(sums.shape) == POS_LANE, 1.0, sums)

    border = border + pltpu.roll(border, 4, 0)
    turned_ref[...] = jnp.concatenate([border] * (LANES // SUB), axis=0).T
    lane = lane_iota((SUB, LANES))
    sides = []
    for side in range(2):
        parts = []
        for part in range(2):
            value = jnp.zeros((SUB, LANES), F32)
            for near in range(HALO):
                column = turned_ref[pl.ds(POS_LANE + 1 + near, SUB, stride=SCENE_LANES), :]
                row = side * 2 + part
                here = lane == (near if side else LANES - HALO + near)
                value = jnp.where(here, column[:, row : row + 1], value)
            parts.append(value)
        sides.append(jnp.concatenate(parts, axis=0))
    sums = jnp.concatenate([sides[0], sums, sides[1]], axis=1)
    width = sums.shape[1]
    rows = [sums[row : row + 1] for row in range(13)]
    matrix = [
        rows[0] + 2.0 * coupling,
        rows[1],
        rows[2],
        rows[3] + 2.0 * coupling,
        rows[4],
        rows[5] + 2.0 * coupling,
    ]
    exists = rows[POS_LANE] > 0.0
    inverse = [jnp.where(exists, entry, 0.0) for entry in inverse_sym(matrix)]

    def apply_pair(vectors):
        return apply_sym(inverse, *vectors[:3]) + apply_sym(inverse, *vectors[3:])

    right_sides = rows[6:12]
    smoothed = apply_pair(right_sides)
    for _ in range(SWEEPS - 1):
        smoothed = apply_pair(
            [
                side + coupling * (pltpu.roll(value, 1, 1) + pltpu.roll(value, width - 1, 1))
                for side, value in zip(right_sides, smoothed)
            ]
        )
    for row in range(6):
        out_ref[row : row + 1, :] = smoothed[row][:, LANES : LANES + scenes]


def call(kernel, out_shape, scratch=(), name=None, vmem=48, **specs):
    return pl.pallas_call(
        kernel,
        out_shape=out_shape,
        scratch_shapes=list(scratch),
        compiler_params=pltpu.CompilerParams(vmem_limit_bytes=vmem * 1024 * 1024),
        name=name,
        **specs,
    )


def shape(dims, dtype=F32):
    return jax.ShapeDtypeStruct(dims, dtype)


def tile_call(got, ground, strips):
    owners = got.shape[0] // BUCKET_ROWS
    tie_rows = owners * 2
    points = ground.shape[1]
    return call(
        functools.partial(tile_kernel, strips=strips),
        (shape(ground.shape), shape((owners * strips, LANES))),
        [
            pltpu.VMEM((9, tie_rows, LANES), F32),
            pltpu.VMEM((2 * SUB * PART_ROWS, LANES), F32),
            pltpu.VMEM((2 * SUB * PART_ROWS, LANES), F32),
            pltpu.VMEM((2, SUB * PART_ROWS, LANES), F32),
            pltpu.VMEM((3 * points // LANES * SUB, LANES), F32),
            pltpu.VMEM((3 * points // LANES, LANES), F32),
            pltpu.VMEM((owners, LANES), F32),
            pltpu.VMEM((owners, LANES), F32),
            pltpu.VMEM((strips * 4, owners // strips + 2 * SUB, LANES), F32),
            pltpu.VMEM((SCENE_ROWS * SCENE_LANES * SUB, LANES), F32),
        ],
        name="tile_sums",
    )(got, ground)


def per_device(
    num_coef,
    den_coef,
    bias,
    scene_chain,
    bucket_scenes,
    tie_counts,
    tie_obs,
    tie_prior,
    tie_pick,
    tie_point,
    ground,
):
    strips = lax.axis_size("strip")
    tiles = lax.axis_size("tile")
    owners = strips * tiles
    tie_dev = tie_prior.shape[0]
    tie_rows = tie_dev // LANES
    scenes_dev = num_coef.shape[1]
    listed = bucket_scenes.shape[1]
    coupling = smooth_gain * (tie_dev // scenes_dev)

    arguments = [
        num_coef,
        den_coef,
        bias,
        scene_chain.reshape(1, scenes_dev),
        bucket_scenes,
        tie_counts,
        tie_obs.reshape(2, tie_rows, LANES).transpose(1, 0, 2).reshape(2 * tie_rows, LANES),
        tie_prior.reshape(tie_rows, LANES),
        tie_pick.reshape(tie_rows, LANES),
        tie_point.reshape(tie_rows, LANES),
    ]
    sent = call(
        pack_kernel,
        shape((owners * BUCKET_ROWS, LANES)),
        [pltpu.VMEM(argument.shape, argument.dtype) for argument in arguments]
        + [
            pltpu.VMEM((LANES, scenes_dev), F32),
            pltpu.VMEM((listed, LANES), F32),
            pltpu.SemaphoreType.DMA((len(arguments),)),
        ],
        name="pack",
        vmem=64,
        in_specs=[pl.BlockSpec(memory_space=pltpu.HBM)] * len(arguments),
    )(*arguments)
    got = lax.all_to_all(
        sent.reshape(owners, BUCKET_ROWS // 2, 2, LANES), AXES, 0, 0, tiled=True
    ).reshape(owners * BUCKET_ROWS, LANES)
    ground_next, totals = tile_call(got, ground, strips)
    got_totals = lax.all_to_all(totals.reshape(owners, strips, LANES), AXES, 0, 0, tiled=True)
    smoothed = call(
        functools.partial(chain_kernel, coupling=coupling),
        shape((6, scenes_dev)),
        [pltpu.VMEM((LANES, LANES), F32)],
        name="chain",
    )(got_totals.reshape(owners * strips, LANES))
    return ground_next, smoothed


def solution(mesh):
    in_specs = (
        P(None, AXES),
        P(None, AXES),
        P(None, AXES),
        P(AXES),
        P(AXES, None),
        P(AXES, None),
        P(None, AXES),
        P(AXES),
        P(AXES),
        P(AXES),
        P(None, AXES),
    )
    out_specs = (P(None, AXES), P(None, AXES))
    return jax.shard_map(
        per_device, mesh=mesh, in_specs=in_specs, out_specs=out_specs, check_vma=False
    )
```

profile of v0, /device:TPU:1, one launch (start us, length us, event | category | flops | bytes accessed | tf_op | source)
XLA Modules:
  0.0 70.2 jit_solution(10893359435065863168)
XLA Ops:
  0.6 3.9 %pack.1 = f32[1792,128]{1,0:T(8,128)} custom-call(bf16[40,512]{1,0:T(8,128)(2,1)} %num_hbm.1, bf16[38,512]{1,0:T(8,128)(2,1)} %den_hbm.1, f32[6,512]{1,0:T(8,128)} %bias_hbm.1, s32[1,512]{1,0:T(1,128)} %bitcast.21, s32[1,1024]{1,0:T(1,128)} %list_hbm.1, s32[1,128]{1,0:T(1,128)} %counts_hbm.1, f32[512,128]{1,0:T(8,128)} %bitcast.17, f32[256,128]{1,0:T(8,128)} %bitcast.18, ...), custom_call_target="tpu_custom_call" | custom-call | tf_op jit(solution)/shard_map/pack/pallas_call | solution.py:681
  4.6 0.0 copy-start
  4.6 29.2 %all_to_all.10 = f32[128,7,2,128]{3,2,1,0:T(2,128)S(1)} all-to-all(f32[128,7,2,128]{3,2,1,0:T(2,128)} %bitcast.16), channel_id=1, replica_groups=mesh['strip'=4,'tile'=32] {'strip','tile'}, dimensions={0} | all-to-all | bytes 1835008 | tf_op jit(solution)/shard_map/all_to_all | solution.py:694
  33.8 0.0 copy-done
  33.8 18.6 %tile_sums.1 = (f32[3,2048]{1,0:T(4,128)}, f32[512,128]{1,0:T(8,128)S(1)}) custom-call(f32[1792,128]{1,0:T(8,128)S(1)} %bitcast.13, f32[3,2048]{1,0:T(4,128)S(1)} %copy-done), custom_call_target="tpu_custom_call" | custom-call | tf_op jit(solution)/shard_map/tile_sums/pallas_call | solution.py:628
  52.4 15.4 %all_to_all.11 = f32[128,4,128]{2,1,0:T(4,128)S(1)} all-to-all(f32[128,4,128]{2,1,0:T(4,128)S(1)} %bitcast.15), channel_id=1, replica_groups=mesh['strip'=4,'tile'=32] {'strip','tile'}, dimensions={0} | all-to-all | bytes 524288 | tf_op jit(solution)/shard_map/all_to_all | solution.py:698
  67.8 2.4 %chain.1 = f32[6,512]{1,0:T(8,128)} custom-call(f32[512,128]{1,0:T(8,128)S(1)} %bitcast.14), custom_call_target="tpu_custom_call" | custom-call | tf_op jit(solution)/shard_map/chain/pallas_call | solution.py:699
Async XLA Ops:
  4.6 29.2 %copy-start = (f32[3,2048]{1,0:T(4,128)S(1)}, f32[3,2048]{1,0:T(4,128)}, u32[]{:S(2)}) copy-start(f32[3,2048]{1,0:T(4,128)} %ground_ref.1) | copy-start | bytes 73732
where the time goes:
time: 70.5 us; the launch traced here: 70.2 us
  blocking collectives  44.6 us (63%)
  Pallas kernels  24.9 us (35%)
    all_to_all x1, blocking collectives, per_device(): lax.all_to_all(sent.reshape(owners, BUCKET_ROWS // 2, 2, LANES), AXES, 0,...  29.2 us
    pallas_call x1, Pallas kernels, tile_call(): call(functools.partial(tile_kernel, strips=strips), (shape(ground.shape),...  18.6 us
    all_to_all x1, blocking collectives, per_device(): lax.all_to_all(totals.reshape(owners, strips, LANES), AXES, 0, 0, tiled=T...  15.4 us
    pallas_call x1, Pallas kernels, per_device(): call(pack_kernel, shape((owners * BUCKET_ROWS, LANES)), [pltpu.VMEM(argum...  3.92 us
    pallas_call x1, Pallas kernels, per_device(): call(functools.partial(chain_kernel, coupling=coupling), shape((6, scenes...  2.43 us

commit v1 on v0

--- a/solution.py
+++ b/solution.py
@@ -24,11 +24,15 @@
 CHAIN_ROW = 104
 CHAIN_SENT = 88
 SCENE_ROWS = 6
+LANE_STEP = 2
 BUCKET_ROWS = 8 + SCENE_ROWS
 SCENE_LANES = 16
 POS_LANE = 12
+TOGETHER = 16
 HALO = SWEEPS - 1
 PART_ROWS = 32
+TERM_ROWS = 20
+BUCKET_PARTS = 68
 
 
 def lane_iota(shape):
@@ -44,6 +48,21 @@
     rest = value - high
     middle = rest.astype(BF16).astype(F32)
     return high, middle, rest - middle
+
+
+def one_hot_rows(low):
+    wide = (16, low.shape[1])
+    held = jnp.broadcast_to(low, wide).astype(BF16)
+    one = jnp.ones(wide, BF16)
+    zero = jnp.zeros(wide, BF16)
+    rows = sublane_iota(wide)
+    return jnp.concatenate(
+        [
+            jnp.where(held == (rows + first).astype(F32).astype(BF16), one, zero)
+            for first in range(0, 256, 16)
+        ],
+        axis=0,
+    )
 
 
 def take_lanes(table, lanes):
@@ -94,7 +113,6 @@
     pick_ref,
     point_ref,
     table_ref,
-    listed_ref,
     sems,
 ):
     copies = [
@@ -137,22 +155,47 @@
     table_ref[CHAIN_ROW : CHAIN_ROW + 1, :] = (place >> 8).astype(F32)
     table_ref[CHAIN_ROW + 1 : CHAIN_ROW + 2, :] = (place & 255).astype(F32)
     table = table_ref[...].astype(BF16)
-    for first in range(0, listed, 256):
-        chosen = jnp.broadcast_to(list_ref[:, first : first + 256], (scenes, 256))
-        onehot = jnp.where(chosen == sublane_iota((scenes, 256)), 1.0, 0.0).astype(BF16)
-        got = jnp.dot(table, onehot, preferred_element_type=F32)
-        bias_rows = sum(
-            got[BIAS_ROW + part * SUB : BIAS_ROW + (part + 1) * SUB] for part in range(1, 3)
-        ) + got[BIAS_ROW : BIAS_ROW + SUB]
-        got = jnp.concatenate([got[:BIAS_ROW], bias_rows, got[CHAIN_ROW:]], axis=0)
-        got = jnp.concatenate([got, jnp.zeros((LANES - got.shape[0], 256), F32)], axis=0)
+    lane = lane_iota((SUB, LANES))
+    per_row = LANES // SUB
+    index = (lane % per_row) * SUB + sublane_iota((SUB, LANES))
+    lists = jnp.zeros((SUB, LANES), F32)
+    for row in range(listed // LANES):
+        ids = list_ref[:, row * LANES : (row + 1) * LANES].astype(F32)
+        found = take_lanes(jnp.broadcast_to(ids, (SUB, LANES)), index)
+        lists = jnp.where(lane // per_row == row, found, lists)
+    lows = []
+    for first in range(0, scenes, 256):
+        inside = (lists >= float(first)) & (lists < float(first + 256))
+        lows.append(jnp.where(inside, lists - float(first), -1.0))
+    got = []
+    for pair in range(0, SUB, 2):
+        onehot = []
+        for k in (pair, pair + 1):
+            onehot.append(
+                jnp.concatenate([one_hot_rows(low[k : k + 1]) for low in lows], axis=0)
+            )
+        both = jnp.dot(
+            table, jnp.concatenate(onehot, axis=1), preferred_element_type=F32
+        )
         for part in range(0, 256, LANES):
-            listed_ref[first + part : first + part + LANES, :] = got[:, part : part + LANES].T
+            one = both[:, part : part + LANES]
+            bias_rows = (
+                one[BIAS_ROW : BIAS_ROW + SUB]
+                + one[BIAS_ROW + SUB : BIAS_ROW + 2 * SUB]
+                + one[BIAS_ROW + 2 * SUB : BIAS_ROW + 3 * SUB]
+            )
+            got.append(jnp.concatenate([one[:BIAS_ROW], bias_rows, one[CHAIN_ROW:]], axis=0))
+    for block in range(SCENE_ROWS):
+        words = slice(block * SCENE_LANES, (block + 1) * SCENE_LANES)
+        turned = jnp.concatenate([one[words] for one in got], axis=0).T
+        for group in range(owners // SUB):
+            out_ref[
+                pl.ds(group * SUB * BUCKET_ROWS + 8 + block, SUB, stride=BUCKET_ROWS), :
+            ] = turned[group * SUB : (group + 1) * SUB]
     for copy in copies[5:]:
         copy.wait()
     counts = jnp.broadcast_to(counts_ref[...].astype(F32), (owners, owners)).T
-    slot = lane_iota((SUB, LANES)).astype(F32)
-    lane = lane_iota((SUB, LANES))
+    slot = lane.astype(F32)
     for group in range(owners // SUB):
         live_count = counts[group * SUB : (group + 1) * SUB, :1]
         base = group * SUB * BUCKET_ROWS
@@ -167,21 +210,6 @@
             live = slot + float(half * LANES) < live_count
             put(4 + half, jnp.where(live, prior_ref[rows, :], 0.0))
             put(6 + half, (pick_ref[rows, :] * 2048 + point_ref[rows, :]).astype(F32))
-        blocks = [listed_ref[pl.ds(group * SUB * 8 + k, SUB, stride=8), :] for k in range(8)]
-        for bit in range(3):
-            step = 1 << bit
-            shift = step * SCENE_LANES
-            odd = ((lane // SCENE_LANES) & step) != 0
-            turned = list(blocks)
-            for k in range(8):
-                if k & step:
-                    continue
-                low, high = blocks[k], blocks[k + step]
-                turned[k] = jnp.where(odd, pltpu.roll(high, shift, 1), low)
-                turned[k + step] = jnp.where(odd, high, pltpu.roll(low, LANES - shift, 1))
-            blocks = turned
-        for block in range(SCENE_ROWS):
-            put(8 + block, blocks[block])
 
 
 def ratios(coef, east, north, up):
@@ -224,13 +252,14 @@
             held = sums[cubic][which]
             sums[cubic][which] = product if held is None else held + product
 
-    bias = []
-    for word in range(SCENE_LANES):
+    words = [w for first in range(LANE_STEP) for w in range(first, SCENE_LANES, LANE_STEP)]
+    bias = [None] * 6
+    for word in words:
         for cubic in range(4):
             add(cubic, word, cubic * SCENE_LANES + word)
         add(word // 4, 16 + word % 4, LATE_TERMS + word)
         if word < 6:
-            bias.append(coef(BIAS_ROW + word))
+            bias[word] = coef(BIAS_ROW + word)
     found = []
     for top, bottom in ((sums[0], sums[2]), (sums[1], sums[3])):
         quotient = top[0] / bottom[0]
@@ -256,6 +285,8 @@
     place_ref,
     halo_ref,
     coef_ref,
+    terms_ref,
+    scene_ref,
     *,
     strips,
 ):
@@ -297,7 +328,7 @@
     def turn_scenes(group):
         for block in range(SCENE_ROWS):
             value = tie_row(group, 8 + block)
-            for word in range(SCENE_LANES if block < 5 else 6):
+            for word in range(0, SCENE_LANES if block < 5 else 6, LANE_STEP):
                 at = (block * SCENE_LANES + word) * SUB
                 coef_ref[at : at + SUB, :] = (
                     pltpu.roll(value, LANES - word, 1) if word else value
@@ -309,7 +340,8 @@
         east, north, up = gather_points(point)
 
         def coef(row):
-            return take_lanes(coef_ref[row * SUB : (row + 1) * SUB, :], first_lane)
+            at = (row - row % LANE_STEP) * SUB
+            return take_lanes(coef_ref[at : at + SUB, :], first_lane + row % LANE_STEP)
 
         line_obs = tie_row(group, 2 * half)
         samp_obs = tie_row(group, 2 * half + 1)
@@ -326,7 +358,7 @@
         sums += [weight * (line_jac[a] * line_res + samp_jac[a] * samp_res) for a in range(3)]
 
         def put(row, value):
-            parts_ref[pl.ds(half * PART_ROWS + row, SUB, stride=2 * PART_ROWS), :] = value
+            parts_ref[pl.ds(half * PART_ROWS + row, SUB, stride=BUCKET_PARTS), :] = value
 
         for row, value in enumerate(sums):
             for part, piece in enumerate(split3(value)):
@@ -341,12 +373,12 @@
     one = jnp.ones(wide, BF16)
     zero = jnp.zeros(wide, BF16)
 
-    def sum_pass(first_bucket, count, parts_ref):
+    def product_of(first_bucket, count, parts_ref):
         left = []
         right = []
         for bucket in range(first_bucket, first_bucket + count):
             for half in range(2):
-                first = (bucket * 2 + half) * PART_ROWS
+                first = bucket * BUCKET_PARTS + half * PART_ROWS
                 values = parts_ref[first : first + PART_ROWS, :].astype(BF16)
                 high = jnp.broadcast_to(parts_ref[first + 27 : first + 28, :], wide).astype(BF16)
                 low = jnp.broadcast_to(parts_ref[first + 28 : first + 29, :], wide).astype(BF16)
@@ -361,21 +393,28 @@
                         [jnp.where(low == step, one, zero) for step in steps_iota], axis=0
                     )
                 )
-        product = lax.dot_general(
+        return lax.dot_general(
             jnp.concatenate(left, axis=1),
             jnp.concatenate(right, axis=1),
             (((1,), (1,)), ((), ())),
             preferred_element_type=F32,
         )
+
+    def sum_pass(first_bucket, count, parts_ref):
+        products = [
+            product_of(first_bucket + part * count // 2, count // 2, parts_ref)
+            for part in range(2)
+        ]
+        product = products[0] + products[1]
         for half in range(2):
             sums_ref[half] += product[:, half * LANES : (half + 1) * LANES]
 
     def both(group, lagging, parts_ref, lagging_ref):
         if group is not None:
             turn_scenes(group)
+        if lagging:
+            sum_pass(0, SUB, lagging_ref)
         for half in range(2):
-            if lagging:
-                sum_pass(half * 4, 4, lagging_ref)
             if group is not None:
                 first_pass(group, half, parts_ref)
 
@@ -422,7 +461,10 @@
         lambda axis, row: step_ref[axis * point_rows + row : axis * point_rows + row + 1, :]
     )
 
-    def second_pass(group, carry):
+    terms_ref[...] = jnp.zeros(terms_ref.shape, F32)
+    scene_ref[...] = jnp.zeros(scene_ref.shape, F32)
+
+    def tie_terms(group, slot):
         rows = []
         picks = []
         for half in range(2):
@@ -458,16 +500,34 @@
                 ]
             )
             picks.append(pick)
-        total = jnp.zeros(vreg, F32)
-        for scene in range(8):
-            first, second = picks[0] == scene, picks[1] == scene
-            for row in range(12):
-                value = jnp.where(first, rows[0][row], 0.0) + jnp.where(second, rows[1][row], 0.0)
-                total = jnp.where(
-                    lane == scene * SCENE_LANES + row,
-                    jnp.sum(value, axis=1, keepdims=True),
-                    total,
-                )
+        for half in range(2):
+            for row, value in enumerate(rows[half] + [picks[half].astype(F32)]):
+                terms_ref[slot * 2 + half, pl.ds(row, SUB, stride=TERM_ROWS), :] = value
+
+    def scene_sums(group, slot):
+        for bucket in range(SUB):
+            chosen = []
+            pieces = [[], [], []]
+            for half in range(2):
+                first = bucket * TERM_ROWS
+                pick = jnp.broadcast_to(
+                    terms_ref[slot * 2 + half, first + 12 : first + 13, :], wide
+                ).astype(BF16)
+                chosen.append(jnp.where(pick == steps_iota[0], one, zero))
+                for part, piece in enumerate(split3(terms_ref[slot * 2 + half, first : first + 16, :])):
+                    pieces[part].append(piece.astype(BF16))
+            scene_ref[slot, bucket * SUB : (bucket + 1) * SUB, :SCENE_LANES] = lax.dot_general(
+                jnp.concatenate(chosen * 3, axis=1),
+                jnp.concatenate(pieces[0] + pieces[1] + pieces[2], axis=1),
+                (((1,), (1,)), ((), ())),
+                preferred_element_type=F32,
+            )[:SUB]
+        total = scene_ref[slot, pl.ds(0, SUB, stride=SUB), :]
+        for scene in range(1, 8):
+            value = pltpu.roll(
+                scene_ref[slot, pl.ds(scene, SUB, stride=SUB), :], scene * SCENE_LANES, 1
+            )
+            total = jnp.where(lane // SCENE_LANES == scene, value, total)
         place = pl.ds(group * SUB, SUB)
         total_ref[place, :] = total
         chain = tie_row(group, 8 + CHAIN_SENT // SCENE_LANES)
@@ -475,9 +535,15 @@
         place_ref[place, :] = take_lanes(chain, chain_lane) * 256.0 + take_lanes(
             chain, chain_lane + 1
         )
+
+    def second_pass(step, carry):
+        for slot in range(TOGETHER):
+            tie_terms(step * TOGETHER + slot, slot)
+        for slot in range(TOGETHER):
+            scene_sums(step * TOGETHER + slot, slot)
         return carry
 
-    lax.fori_loop(0, groups, second_pass, 0, unroll=2)
+    lax.fori_loop(0, groups // TOGETHER, second_pass, 0)
 
     segment = 4 * LANES
     word = lane % SCENE_LANES
@@ -538,7 +604,9 @@
 
 def chain_kernel(got_ref, out_ref, turned_ref, *, coupling):
     scenes = out_ref.shape[1]
-    total = jnp.zeros((3 * SCENE_LANES, scenes), F32)
+    parts = scenes // 256
+    part_rows = 3 * SCENE_LANES
+    total = jnp.zeros((parts * part_rows, 256), F32)
     border = jnp.zeros((SUB, LANES), F32)
     for first in range(0, got_ref.shape[0], LANES):
         block = got_ref[first : first + LANES, :]
@@ -548,17 +616,29 @@
         values = jnp.concatenate(
             [turned[k * SCENE_LANES : (k + 1) * SCENE_LANES] for k in range(8)], axis=1
         )
-        position = values[POS_LANE : POS_LANE + 1].astype(I32)
-        onehot = jnp.where(
-            jnp.broadcast_to(position, (scenes, 8 * LANES)) == sublane_iota((scenes, 8 * LANES)),
-            1.0,
-            0.0,
-        ).astype(BF16)
-        pieces = jnp.concatenate(split3(values), axis=0).astype(BF16)
+        position = values[POS_LANE : POS_LANE + 1]
+        part_of = (position * (1.0 / 256.0)).astype(I32).astype(F32)
+        held = jnp.broadcast_to(part_of, values.shape).astype(BF16)
+        pieces = [piece.astype(BF16) for piece in split3(values)]
+        zero = jnp.zeros(values.shape, BF16)
+        left = [
+            jnp.where(held == jnp.full(values.shape, part, BF16), piece, zero)
+            for part in range(parts)
+            for piece in pieces
+        ]
         total = total + lax.dot_general(
-            pieces, onehot, (((1,), (1,)), ((), ())), preferred_element_type=F32
+            jnp.concatenate(left, axis=0),
+            one_hot_rows(position - 256.0 * part_of),
+            (((1,), (1,)), ((), ())),
+            preferred_element_type=F32,
         )
-    sums = total[32:48] + total[16:32] + total[:16]
+    sums = jnp.concatenate(
+        [
+            total[first + 32 : first + 48] + total[first + 16 : first + 32] + total[first : first + 16]
+            for first in range(0, parts * part_rows, part_rows)
+        ],
+        axis=1,
+    )
     sums = jnp.where(sublane_iota(sums.shape) == POS_LANE, 1.0, sums)
 
     border = border + pltpu.roll(border, 4, 0)
@@ -630,8 +710,8 @@
         (shape(ground.shape), shape((owners * strips, LANES))),
         [
             pltpu.VMEM((9, tie_rows, LANES), F32),
-            pltpu.VMEM((2 * SUB * PART_ROWS, LANES), F32),
-            pltpu.VMEM((2 * SUB * PART_ROWS, LANES), F32),
+            pltpu.VMEM((SUB * BUCKET_PARTS, LANES), F32),
+            pltpu.VMEM((SUB * BUCKET_PARTS, LANES), F32),
             pltpu.VMEM((2, SUB * PART_ROWS, LANES), F32),
             pltpu.VMEM((3 * points // LANES * SUB, LANES), F32),
             pltpu.VMEM((3 * points // LANES, LANES), F32),
@@ -639,6 +719,8 @@
             pltpu.VMEM((owners, LANES), F32),
             pltpu.VMEM((strips * 4, owners // strips + 2 * SUB, LANES), F32),
             pltpu.VMEM((SCENE_ROWS * SCENE_LANES * SUB, LANES), F32),
+            pltpu.VMEM((2 * TOGETHER, SUB * TERM_ROWS, LANES), F32),
+            pltpu.VMEM((TOGETHER, SUB * SUB, LANES), F32),
         ],
         name="tile_sums",
     )(got, ground)
@@ -663,7 +745,6 @@
     tie_dev = tie_prior.shape[0]
     tie_rows = tie_dev // LANES
     scenes_dev = num_coef.shape[1]
-    listed = bucket_scenes.shape[1]
     coupling = smooth_gain * (tie_dev // scenes_dev)
 
     arguments = [
@@ -683,8 +764,7 @@
         shape((owners * BUCKET_ROWS, LANES)),
         [pltpu.VMEM(argument.shape, argument.dtype) for argument in arguments]
         + [
-            pltpu.VMEM((LANES, scenes_dev), F32),
-            pltpu.VMEM((listed, LANES), F32),
+            pltpu.VMEM((CHAIN_ROW + SUB, scenes_dev), F32),
             pltpu.SemaphoreType.DMA((len(arguments),)),
         ],
         name="pack",

time: 70.5 us -> 63 us (0.89)
  Pallas kernels: 24.9 us -> 17.4 us
    pallas_call x1, Pallas kernels: 18.6 us -> 13.1 us  [tile_call(): call(functools.partial(tile_kernel, strips=strips), (shape(ground.shape),...]
    pallas_call x1, Pallas kernels: 3.92 us -> 2.51 us  [per_device(): call(pack_kernel, shape((owners * BUCKET_ROWS, LANES)), [pltpu.VMEM(argum...]
where the time goes in v1:
time: 63 us; the launch traced here: 62.7 us
  blocking collectives  44.6 us (71%)
  Pallas kernels  17.4 us (28%)
  between operations  0.66 us (1%)
    all_to_all x1, blocking collectives, per_device(): lax.all_to_all(sent.reshape(owners, BUCKET_ROWS // 2, 2, LANES), AXES, 0,...  29.2 us
    all_to_all x1, blocking collectives, per_device(): lax.all_to_all(totals.reshape(owners, strips, LANES), AXES, 0, 0, tiled=T...  15.4 us
    pallas_call x1, Pallas kernels, tile_call(): call(functools.partial(tile_kernel, strips=strips), (shape(ground.shape),...  13.1 us
    pallas_call x1, Pallas kernels, per_device(): call(pack_kernel, shape((owners * BUCKET_ROWS, LANES)), [pltpu.VMEM(argum...  2.51 us
    pallas_call x1, Pallas kernels, per_device(): call(functools.partial(chain_kernel, coupling=coupling), shape((6, scenes...  1.84 us

profile of v1, /device:TPU:1, one launch (start us, length us, event | category | flops | bytes accessed | tf_op | source)
XLA Modules:
  0.0 62.7 jit_solution(17719679681981516651)
XLA Ops:
  0.6 2.5 %pack.1 = f32[1792,128]{1,0:T(8,128)} custom-call(bf16[40,512]{1,0:T(8,128)(2,1)} %num_hbm.1, bf16[38,512]{1,0:T(8,128)(2,1)} %den_hbm.1, f32[6,512]{1,0:T(8,128)} %bias_hbm.1, s32[1,512]{1,0:T(1,128)} %bitcast.21, s32[1,1024]{1,0:T(1,128)} %list_hbm.1, s32[1,128]{1,0:T(1,128)} %counts_hbm.1, f32[512,128]{1,0:T(8,128)} %bitcast.17, f32[256,128]{1,0:T(8,128)} %bitcast.18, ...), custom_call_target="tpu_custom_call" | custom-call | tf_op jit(solution)/shard_map/pack/pallas_call | solution.py:762
  3.2 0.0 copy-start
  3.2 29.2 %all_to_all.10 = f32[128,7,2,128]{3,2,1,0:T(2,128)S(1)} all-to-all(f32[128,7,2,128]{3,2,1,0:T(2,128)} %bitcast.16), channel_id=1, replica_groups=mesh['strip'=4,'tile'=32] {'strip','tile'}, dimensions={0} | all-to-all | bytes 1835008 | tf_op jit(solution)/shard_map/all_to_all | solution.py:774
  32.4 0.0 copy-done
  32.4 13.1 %tile_sums.1 = (f32[3,2048]{1,0:T(4,128)}, f32[512,128]{1,0:T(8,128)S(1)}) custom-call(f32[1792,128]{1,0:T(8,128)S(1)} %bitcast.13, f32[3,2048]{1,0:T(4,128)S(1)} %copy-done), custom_call_target="tpu_custom_call" | custom-call | tf_op jit(solution)/shard_map/tile_sums/pallas_call | solution.py:708
  45.5 15.4 %all_to_all.11 = f32[128,4,128]{2,1,0:T(4,128)S(1)} all-to-all(f32[128,4,128]{2,1,0:T(4,128)S(1)} %bitcast.15), channel_id=1, replica_groups=mesh['strip'=4,'tile'=32] {'strip','tile'}, dimensions={0} | all-to-all | bytes 524288 | tf_op jit(solution)/shard_map/all_to_all | solution.py:778
  60.9 1.8 %chain.1 = f32[6,512]{1,0:T(8,128)} custom-call(f32[512,128]{1,0:T(8,128)S(1)} %bitcast.14), custom_call_target="tpu_custom_call" | custom-call | tf_op jit(solution)/shard_map/chain/pallas_call | solution.py:779
Async XLA Ops:
  3.2 29.2 %copy-start = (f32[3,2048]{1,0:T(4,128)S(1)}, f32[3,2048]{1,0:T(4,128)}, u32[]{:S(2)}) copy-start(f32[3,2048]{1,0:T(4,128)} %ground_ref.1) | copy-start | bytes 73732

commit v2 on v1

--- a/solution.py
+++ b/solution.py
@@ -29,8 +29,10 @@
 SCENE_LANES = 16
 POS_LANE = 12
 TOGETHER = 16
+BUFFERS = 2
 HALO = SWEEPS - 1
 PART_ROWS = 32
+SUM_ROWS = 36
 TERM_ROWS = 20
 BUCKET_PARTS = 68
 
@@ -276,8 +278,7 @@
     next_ref,
     out_ref,
     packed_ref,
-    parts_even,
-    parts_odd,
+    parts_ref,
     sums_ref,
     table_ref,
     step_ref,
@@ -330,18 +331,20 @@
             value = tie_row(group, 8 + block)
             for word in range(0, SCENE_LANES if block < 5 else 6, LANE_STEP):
                 at = (block * SCENE_LANES + word) * SUB
-                coef_ref[at : at + SUB, :] = (
+                coef_ref[group % BUFFERS, at : at + SUB, :] = (
                     pltpu.roll(value, LANES - word, 1) if word else value
                 )
 
-    def first_pass(group, half, parts_ref):
+    def first_pass(group, half):
         pick, point = code_of(group, half)
         first_lane = pick * SCENE_LANES
         east, north, up = gather_points(point)
 
         def coef(row):
             at = (row - row % LANE_STEP) * SUB
-            return take_lanes(coef_ref[at : at + SUB, :], first_lane + row % LANE_STEP)
+            return take_lanes(
+                coef_ref[group % BUFFERS, at : at + SUB, :], first_lane + row % LANE_STEP
+            )
 
         line_obs = tie_row(group, 2 * half)
         samp_obs = tie_row(group, 2 * half + 1)
@@ -358,7 +361,9 @@
         sums += [weight * (line_jac[a] * line_res + samp_jac[a] * samp_res) for a in range(3)]
 
         def put(row, value):
-            parts_ref[pl.ds(half * PART_ROWS + row, SUB, stride=BUCKET_PARTS), :] = value
+            parts_ref[
+                group % BUFFERS, pl.ds(half * PART_ROWS + row, SUB, stride=BUCKET_PARTS), :
+            ] = value
 
         for row, value in enumerate(sums):
             for part, piece in enumerate(split3(value)):
@@ -373,15 +378,16 @@
     one = jnp.ones(wide, BF16)
     zero = jnp.zeros(wide, BF16)
 
-    def product_of(first_bucket, count, parts_ref):
+    def product_of(group, first_bucket, count):
+        held = parts_ref.at[group % BUFFERS]
         left = []
         right = []
         for bucket in range(first_bucket, first_bucket + count):
             for half in range(2):
                 first = bucket * BUCKET_PARTS + half * PART_ROWS
-                values = parts_ref[first : first + PART_ROWS, :].astype(BF16)
-                high = jnp.broadcast_to(parts_ref[first + 27 : first + 28, :], wide).astype(BF16)
-                low = jnp.broadcast_to(parts_ref[first + 28 : first + 29, :], wide).astype(BF16)
+                values = held[first : first + PART_ROWS, :].astype(BF16)
+                high = jnp.broadcast_to(held[first + 27 : first + 28, :], wide).astype(BF16)
+                low = jnp.broadcast_to(held[first + 28 : first + 29, :], wide).astype(BF16)
                 rows = []
                 for index in range(8):
                     here = high == jnp.full(wide, index, BF16)
@@ -400,41 +406,31 @@
             preferred_element_type=F32,
         )
 
-    def sum_pass(first_bucket, count, parts_ref):
+    def sum_pass(group, first_bucket, count):
         products = [
-            product_of(first_bucket + part * count // 2, count // 2, parts_ref)
+            product_of(group, first_bucket + part * count // 2, count // 2)
             for part in range(2)
         ]
         product = products[0] + products[1]
         for half in range(2):
-            sums_ref[half] += product[:, half * LANES : (half + 1) * LANES]
-
-    def both(group, lagging, parts_ref, lagging_ref):
-        if group is not None:
+            for index in range(SUB):
+                held = slice(index * SUM_ROWS, index * SUM_ROWS + PART_ROWS)
+                rows = slice(index * PART_ROWS, (index + 1) * PART_ROWS)
+                sums_ref[half, held, :] += product[rows, half * LANES : (half + 1) * LANES]
+
+    sums_ref[...] = jnp.zeros(sums_ref.shape, F32)
+    for group in range(groups + 1):
+        if group < groups:
             turn_scenes(group)
-        if lagging:
-            sum_pass(0, SUB, lagging_ref)
-        for half in range(2):
-            if group is not None:
-                first_pass(group, half, parts_ref)
-
-    for ref in (parts_even, parts_odd):
-        ref[...] = jnp.zeros(ref.shape, F32)
-    sums_ref[...] = jnp.zeros(sums_ref.shape, F32)
-    both(0, False, parts_even, None)
-
-    def pair_of_groups(pair, carry):
-        both(2 * pair + 1, True, parts_odd, parts_even)
-        both(2 * pair + 2, True, parts_even, parts_odd)
-        return carry
-
-    lax.fori_loop(0, groups // 2 - 1, pair_of_groups, 0)
-    both(groups - 1, True, parts_odd, parts_even)
-    both(None, True, None, parts_odd)
+        if group:
+            sum_pass(group - 1, 0, SUB)
+        if group < groups:
+            for half in range(2):
+                first_pass(group, half)
 
     def point_sum(row, half):
         return sum(
-            sums_ref[half, pl.ds(row * 3 + part, SUB, stride=PART_ROWS), :] for part in (2, 1, 0)
+            sums_ref[half, pl.ds(row * 3 + part, SUB, stride=SUM_ROWS), :] for part in (2, 1, 0)
         )
 
     for half in range(2):
@@ -460,9 +456,6 @@
     fill_table(
         lambda axis, row: step_ref[axis * point_rows + row : axis * point_rows + row + 1, :]
     )
-
-    terms_ref[...] = jnp.zeros(terms_ref.shape, F32)
-    scene_ref[...] = jnp.zeros(scene_ref.shape, F32)
 
     def tie_terms(group, slot):
         rows = []
@@ -501,7 +494,8 @@
             )
             picks.append(pick)
         for half in range(2):
-            for row, value in enumerate(rows[half] + [picks[half].astype(F32)]):
+            spare = [jnp.zeros(vreg, F32)] * 3
+            for row, value in enumerate(rows[half] + [picks[half].astype(F32)] + spare):
                 terms_ref[slot * 2 + half, pl.ds(row, SUB, stride=TERM_ROWS), :] = value
 
     def scene_sums(group, slot):
@@ -602,7 +596,7 @@
                 ] = value
 
 
-def chain_kernel(got_ref, out_ref, turned_ref, *, coupling):
+def chain_kernel(got_ref, out_ref, turned_ref, joined_ref, *, coupling):
     scenes = out_ref.shape[1]
     parts = scenes // 256
     part_rows = 3 * SCENE_LANES
@@ -658,7 +652,8 @@
         sides.append(jnp.concatenate(parts, axis=0))
     sums = jnp.concatenate([sides[0], sums, sides[1]], axis=1)
     width = sums.shape[1]
-    rows = [sums[row : row + 1] for row in range(13)]
+    joined_ref[...] = sums
+    rows = [joined_ref[row : row + 1, :] for row in range(6)]
     matrix = [
         rows[0] + 2.0 * coupling,
         rows[1],
@@ -667,23 +662,31 @@
         rows[4],
         rows[5] + 2.0 * coupling,
     ]
-    exists = rows[POS_LANE] > 0.0
-    inverse = [jnp.where(exists, entry, 0.0) for entry in inverse_sym(matrix)]
-
-    def apply_pair(vectors):
-        return apply_sym(inverse, *vectors[:3]) + apply_sym(inverse, *vectors[3:])
-
-    right_sides = rows[6:12]
-    smoothed = apply_pair(right_sides)
+    exists = joined_ref[POS_LANE : POS_LANE + 1, :] > 0.0
+    inverse = [
+        jnp.broadcast_to(jnp.where(exists, entry, 0.0), (2, width))
+        for entry in inverse_sym(matrix)
+    ]
+    right_sides = [
+        jnp.concatenate(
+            [joined_ref[6 + term : 7 + term, :], joined_ref[9 + term : 10 + term, :]], axis=0
+        )
+        for term in range(3)
+    ]
+    smoothed = apply_sym(inverse, *right_sides)
     for _ in range(SWEEPS - 1):
-        smoothed = apply_pair(
-            [
+        smoothed = apply_sym(
+            inverse,
+            *[
                 side + coupling * (pltpu.roll(value, 1, 1) + pltpu.roll(value, width - 1, 1))
                 for side, value in zip(right_sides, smoothed)
+            ],
+        )
+    for term in range(3):
+        for row in range(2):
+            out_ref[3 * row + term : 3 * row + term + 1, :] = smoothed[term][
+                row : row + 1, LANES : LANES + scenes
             ]
-        )
-    for row in range(6):
-        out_ref[row : row + 1, :] = smoothed[row][:, LANES : LANES + scenes]
 
 
 def call(kernel, out_shape, scratch=(), name=None, vmem=48, **specs):
@@ -710,15 +713,14 @@
         (shape(ground.shape), shape((owners * strips, LANES))),
         [
             pltpu.VMEM((9, tie_rows, LANES), F32),
-            pltpu.VMEM((SUB * BUCKET_PARTS, LANES), F32),
-            pltpu.VMEM((SUB * BUCKET_PARTS, LANES), F32),
-            pltpu.VMEM((2, SUB * PART_ROWS, LANES), F32),
+            pltpu.VMEM((BUFFERS, SUB * BUCKET_PARTS, LANES), F32),
+            pltpu.VMEM((2, SUB * SUM_ROWS, LANES), F32),
             pltpu.VMEM((3 * points // LANES * SUB, LANES), F32),
             pltpu.VMEM((3 * points // LANES, LANES), F32),
             pltpu.VMEM((owners, LANES), F32),
             pltpu.VMEM((owners, LANES), F32),
             pltpu.VMEM((strips * 4, owners // strips + 2 * SUB, LANES), F32),
-            pltpu.VMEM((SCENE_ROWS * SCENE_LANES * SUB, LANES), F32),
+            pltpu.VMEM((BUFFERS, SCENE_ROWS * SCENE_LANES * SUB, LANES), F32),
             pltpu.VMEM((2 * TOGETHER, SUB * TERM_ROWS, LANES), F32),
             pltpu.VMEM((TOGETHER, SUB * SUB, LANES), F32),
         ],
@@ -779,7 +781,7 @@
     smoothed = call(
         functools.partial(chain_kernel, coupling=coupling),
         shape((6, scenes_dev)),
-        [pltpu.VMEM((LANES, LANES), F32)],
+        [pltpu.VMEM((LANES, LANES), F32), pltpu.VMEM((16, scenes_dev + 2 * LANES), F32)],
         name="chain",
     )(got_totals.reshape(owners * strips, LANES))
     return ground_next, smoothed

time: 63 us -> 61.8 us (0.981)
  Pallas kernels: 17.4 us -> 16.3 us
    pallas_call x1, Pallas kernels: 13.1 us -> 11.9 us  [tile_call(): call(functools.partial(tile_kernel, strips=strips), (shape(ground.shape),...]
where the time goes in v2:
time: 61.8 us; the launch traced here: 61.6 us
  blocking collectives  44.6 us (72%)
  Pallas kernels  16.3 us (26%)
  between operations  0.66 us (1%)
    all_to_all x1, blocking collectives, per_device(): lax.all_to_all(sent.reshape(owners, BUCKET_ROWS // 2, 2, LANES), AXES, 0,...  29.2 us
    all_to_all x1, blocking collectives, per_device(): lax.all_to_all(totals.reshape(owners, strips, LANES), AXES, 0, 0, tiled=T...  15.4 us
    pallas_call x1, Pallas kernels, tile_call(): call(functools.partial(tile_kernel, strips=strips), (shape(ground.shape),...  11.9 us
    pallas_call x1, Pallas kernels, per_device(): call(pack_kernel, shape((owners * BUCKET_ROWS, LANES)), [pltpu.VMEM(argum...  2.51 us
    pallas_call x1, Pallas kernels, per_device(): call(functools.partial(chain_kernel, coupling=coupling), shape((6, scenes...  1.83 us

profile of v2, /device:TPU:1, one launch (start us, length us, event | category | flops | bytes accessed | tf_op | source)
XLA Modules:
  0.0 61.6 jit_solution(333509029594565355)
XLA Ops:
  0.6 2.5 %pack.1 = f32[1792,128]{1,0:T(8,128)} custom-call(bf16[40,512]{1,0:T(8,128)(2,1)} %num_hbm.1, bf16[38,512]{1,0:T(8,128)(2,1)} %den_hbm.1, f32[6,512]{1,0:T(8,128)} %bias_hbm.1, s32[1,512]{1,0:T(1,128)} %bitcast.21, s32[1,1024]{1,0:T(1,128)} %list_hbm.1, s32[1,128]{1,0:T(1,128)} %counts_hbm.1, f32[512,128]{1,0:T(8,128)} %bitcast.17, f32[256,128]{1,0:T(8,128)} %bitcast.18, ...), custom_call_target="tpu_custom_call" | custom-call | tf_op jit(solution)/shard_map/pack/pallas_call | solution.py:764
  3.2 0.0 copy-start
  3.2 29.2 %all_to_all.10 = f32[128,7,2,128]{3,2,1,0:T(2,128)S(1)} all-to-all(f32[128,7,2,128]{3,2,1,0:T(2,128)} %bitcast.16), channel_id=1, replica_groups=mesh['strip'=4,'tile'=32] {'strip','tile'}, dimensions={0} | all-to-all | bytes 1835008 | tf_op jit(solution)/shard_map/all_to_all | solution.py:776
  32.4 0.0 copy-done
  32.4 11.9 %tile_sums.1 = (f32[3,2048]{1,0:T(4,128)}, f32[512,128]{1,0:T(8,128)S(1)}) custom-call(f32[1792,128]{1,0:T(8,128)S(1)} %bitcast.13, f32[3,2048]{1,0:T(4,128)S(1)} %copy-done), custom_call_target="tpu_custom_call" | custom-call | tf_op jit(solution)/shard_map/tile_sums/pallas_call | solution.py:711
  44.3 15.4 %all_to_all.11 = f32[128,4,128]{2,1,0:T(4,128)S(1)} all-to-all(f32[128,4,128]{2,1,0:T(4,128)S(1)} %bitcast.15), channel_id=1, replica_groups=mesh['strip'=4,'tile'=32] {'strip','tile'}, dimensions={0} | all-to-all | bytes 524288 | tf_op jit(solution)/shard_map/all_to_all | solution.py:780
  59.7 1.8 %chain.1 = f32[6,512]{1,0:T(8,128)} custom-call(f32[512,128]{1,0:T(8,128)S(1)} %bitcast.14), custom_call_target="tpu_custom_call" | custom-call | tf_op jit(solution)/shard_map/chain/pallas_call | solution.py:781
Async XLA Ops:
  3.2 29.2 %copy-start = (f32[3,2048]{1,0:T(4,128)S(1)}, f32[3,2048]{1,0:T(4,128)}, u32[]{:S(2)}) copy-start(f32[3,2048]{1,0:T(4,128)} %ground_ref.1) | copy-start | bytes 73732

commit v3 on v2

--- a/solution.py
+++ b/solution.py
@@ -317,13 +317,17 @@
     def gather_points(point):
         high = point >> 7
         low = point & (LANES - 1)
-        found = [None] * 3
-        for row in range(point_rows):
-            here = high == row
-            for axis in range(3):
-                at = (axis * point_rows + row) * SUB
-                value = take_lanes(table_ref[at : at + SUB, :], low)
-                found[axis] = value if row == 0 else jnp.where(here, value, found[axis])
+        bits = [(high & (1 << bit)) != 0 for bit in range((point_rows - 1).bit_length())]
+
+        def pick(axis, first, bit):
+            if bit < 0:
+                at = (axis * point_rows + first) * SUB
+                return take_lanes(table_ref[at : at + SUB, :], low)
+            return jnp.where(
+                bits[bit], pick(axis, first + (1 << bit), bit - 1), pick(axis, first, bit - 1)
+            )
+
+        found = [pick(axis, 0, len(bits) - 1) for axis in range(3)]
         return found
 
     def turn_scenes(group):

time: 61.8 us -> 61.5 us (level)
  no operation moved by 1% of the time
where the time goes in v3:
time: 61.5 us; the launch traced here: 61.2 us
  blocking collectives  44.6 us (73%)
  Pallas kernels  16 us (26%)
  between operations  0.66 us (1%)
    all_to_all x1, blocking collectives, per_device(): lax.all_to_all(sent.reshape(owners, BUCKET_ROWS // 2, 2, LANES), AXES, 0,...  29.2 us
    all_to_all x1, blocking collectives, per_device(): lax.all_to_all(totals.reshape(owners, strips, LANES), AXES, 0, 0, tiled=T...  15.4 us
    pallas_call x1, Pallas kernels, tile_call(): call(functools.partial(tile_kernel, strips=strips), (shape(ground.shape),...  11.6 us
    pallas_call x1, Pallas kernels, per_device(): call(pack_kernel, shape((owners * BUCKET_ROWS, LANES)), [pltpu.VMEM(argum...  2.51 us
    pallas_call x1, Pallas kernels, per_device(): call(functools.partial(chain_kernel, coupling=coupling), shape((6, scenes...  1.83 us

profile of v3, /device:TPU:1, one launch (start us, length us, event | category | flops | bytes accessed | tf_op | source)
XLA Modules:
  0.0 61.2 jit_solution(16110887621001342020)
XLA Ops:
  0.6 2.5 %pack.1 = f32[1792,128]{1,0:T(8,128)} custom-call(bf16[40,512]{1,0:T(8,128)(2,1)} %num_hbm.1, bf16[38,512]{1,0:T(8,128)(2,1)} %den_hbm.1, f32[6,512]{1,0:T(8,128)} %bias_hbm.1, s32[1,512]{1,0:T(1,128)} %bitcast.21, s32[1,1024]{1,0:T(1,128)} %list_hbm.1, s32[1,128]{1,0:T(1,128)} %counts_hbm.1, f32[512,128]{1,0:T(8,128)} %bitcast.17, f32[256,128]{1,0:T(8,128)} %bitcast.18, ...), custom_call_target="tpu_custom_call" | custom-call | tf_op jit(solution)/shard_map/pack/pallas_call | solution.py:768
  3.2 0.0 copy-start
  3.2 29.2 %all_to_all.10 = f32[128,7,2,128]{3,2,1,0:T(2,128)S(1)} all-to-all(f32[128,7,2,128]{3,2,1,0:T(2,128)} %bitcast.16), channel_id=1, replica_groups=mesh['strip'=4,'tile'=32] {'strip','tile'}, dimensions={0} | all-to-all | bytes 1835008 | tf_op jit(solution)/shard_map/all_to_all | solution.py:780
  32.4 0.0 copy-done
  32.4 11.6 %tile_sums.1 = (f32[3,2048]{1,0:T(4,128)}, f32[512,128]{1,0:T(8,128)S(1)}) custom-call(f32[1792,128]{1,0:T(8,128)S(1)} %bitcast.13, f32[3,2048]{1,0:T(4,128)S(1)} %copy-done), custom_call_target="tpu_custom_call" | custom-call | tf_op jit(solution)/shard_map/tile_sums/pallas_call | solution.py:715
  44.0 15.4 %all_to_all.11 = f32[128,4,128]{2,1,0:T(4,128)S(1)} all-to-all(f32[128,4,128]{2,1,0:T(4,128)S(1)} %bitcast.15), channel_id=1, replica_groups=mesh['strip'=4,'tile'=32] {'strip','tile'}, dimensions={0} | all-to-all | bytes 524288 | tf_op jit(solution)/shard_map/all_to_all | solution.py:784
  59.4 1.8 %chain.1 = f32[6,512]{1,0:T(8,128)} custom-call(f32[512,128]{1,0:T(8,128)S(1)} %bitcast.14), custom_call_target="tpu_custom_call" | custom-call | tf_op jit(solution)/shard_map/chain/pallas_call | solution.py:785
Async XLA Ops:
  3.2 29.2 %copy-start = (f32[3,2048]{1,0:T(4,128)S(1)}, f32[3,2048]{1,0:T(4,128)}, u32[]{:S(2)}) copy-start(f32[3,2048]{1,0:T(4,128)} %ground_ref.1) | copy-start | bytes 73732
